TPU v7x, 32 devices: a whole 2x2x4 slice. The times are simulated.
32 devices in a mesh: groups: 2 (over y), branch: 4 (over z), dp: 2 (over x), mp: 2 (over core).
Axes of the slice: x: 2, y: 2, z: 4, core: 2. Of those that a mesh axis runs over, the one named last changes fastest.
Arguments:
- queries: bfloat16 [4, 4, 384, 4096], P(('groups', 'dp'), 'branch', None, 'mp'), parts along dimension 0, may hold values from -160 to 160
- own_kv: bfloat16 [4, 4, 2, 384, 512], P(('groups', 'dp'), 'branch', None, None, 'mp'), parts along dimension 0, may hold values from -6 to 6
- segment_key_values: bfloat16 [4, 4, 3, 2, 128, 512], P(('groups', 'dp'), 'branch', None, None, None, 'mp'), parts along dimension 0, may hold values from -6 to 6
- ancestors: int32 [4, 4, 3], P(('groups', 'dp'), 'branch'), parts along dimension 0, may hold values from 0 to 3, as said below
- seg_tiles: int32 [4, 4, 3], P(('groups', 'dp'), 'branch'), parts along dimension 0, may hold values from 1 to 2, as said below
- grad_out: bfloat16 [4, 4, 384, 4096], P(('groups', 'dp'), 'branch', None, 'mp'), parts along dimension 0, may hold values from -6 to 6
Outputs:
- attn_out: bfloat16 [4, 4, 384, 4096], P(('groups', 'dp'), 'branch', None, 'mp'), parts along dimension 0
- d_queries: bfloat16 [4, 4, 384, 4096], P(('groups', 'dp'), 'branch', None, 'mp'), parts along dimension 0
- branch_key_value_gradient: float32 [4, 4, 2, 384, 512], P(('groups', 'dp'), 'branch', None, None, 'mp'), parts along dimension 0
- d_seg_kv: float32 [4, 4, 3, 2, 128, 512], P(('groups', 'dp'), 'branch', None, None, None, 'mp'), parts along dimension 0
There are 2 independent parts, one for each index of `groups`. A program takes and returns all parts, laid end to end along the dimension named above; each array names one. Nothing has to cross between parts.
Inputs may be any that keep to these rules, and one draw needn't show every extreme that they name: ancestors[p, b, 0] = 0; at each level the branches with ancestor h form one contiguous run that begins at branch h, and each level's runs split those of the level before. `seg_tiles`: the segment that branch 0 stores for level 0 has 2 tiles.
All inputs are finite; a program needn't handle non-finite values.
Results may differ from a plain program's by a relative error of at most 0.035.
Values may be sent and summed in bfloat16 or wider, within the bound.
A program may use at most 128 MiB of HBM per device.

v0:
```python
import jax
import jax.numpy as jnp
from jax import lax
from jax.sharding import PartitionSpec as P

QUERY_HEAD_COUNT = 32
KEY_VALUE_HEADS = 4
HEAD_DIMENSION = 128
TILE = 64


def local(queries, own_kv, segment_key_values, ancestors, seg_tiles, grad_out):
    lineage = ancestors[0, 0]
    held_slots = segment_key_values[0, 0]
    levels = held_slots.shape[0]
    seg_len = held_slots.shape[2]
    kv_width = held_slots.shape[3]
    held_kv = jnp.zeros_like(held_slots)
    held_tiles = jnp.zeros((levels,), jnp.bfloat16)
    part_kv = lax.all_gather(segment_key_values, "branch", axis=1, tiled=True)
    part_tiles = lax.all_gather(seg_tiles.astype(jnp.bfloat16), "branch", axis=1, tiled=True)
    span_rows = part_kv.shape[1]
    new_kv = []
    new_tiles = []
    for depth_level in range(levels):
        offset = lineage[depth_level]
        inside = (offset >= 0) & (offset < span_rows)
        safe_row = jnp.clip(offset, 0, span_rows - 1)
        chosen_kv = lax.dynamic_index_in_dim(
            part_kv[0, :, depth_level], safe_row, 0, keepdims=False
        )
        chosen_tiles = lax.dynamic_index_in_dim(
            part_tiles[0, :, depth_level], safe_row, 0, keepdims=False
        )
        new_kv.append(jnp.where(inside, chosen_kv, held_kv[depth_level]))
        new_tiles.append(jnp.where(inside, chosen_tiles, held_tiles[depth_level]))
    fetched_kv = jnp.stack(new_kv)
    fetched_tiles = jnp.stack(new_tiles)
    tile_counts = fetched_tiles.astype(jnp.int32)
    own_pair = own_kv[0, 0]
    own_len = own_pair.shape[1]
    shared_prefix_length = levels * seg_len
    every_key_row = jnp.concatenate(
        [fetched_kv[:, 0].reshape(shared_prefix_length, kv_width), own_pair[0]], axis=0
    )
    every_value_row = jnp.concatenate(
        [fetched_kv[:, 1].reshape(shared_prefix_length, kv_width), own_pair[1]], axis=0
    )
    positions = jnp.arange(seg_len)
    prefix_ok = (positions[None, :] < (tile_counts * TILE)[:, None]).reshape(shared_prefix_length)
    own_rows = jnp.arange(own_len)
    causal = own_rows[None, :] <= own_rows[:, None]
    allowed = jnp.concatenate(
        [jnp.broadcast_to(prefix_ok[None, :], (own_len, shared_prefix_length)), causal], axis=1
    )
    score_scale = HEAD_DIMENSION ** (-0.5)
    query_group_width = QUERY_HEAD_COUNT // KEY_VALUE_HEADS
    query_row_block = queries[0, 0]
    gradient_row_block = grad_out[0, 0]
    out_blocks = []
    query_grads = []
    key_grads = []
    value_grads = []
    for kv_head in range(kv_width // HEAD_DIMENSION):
        head_cols = slice(
            kv_head * query_group_width * HEAD_DIMENSION,
            (kv_head + 1) * query_group_width * HEAD_DIMENSION,
        )
        query_head_block = query_row_block[:, head_cols].reshape(
            own_len, query_group_width, HEAD_DIMENSION
        )
        gradient_per_head = gradient_row_block[:, head_cols].reshape(
            own_len, query_group_width, HEAD_DIMENSION
        )
        key_head = every_key_row[:, kv_head * HEAD_DIMENSION : (kv_head + 1) * HEAD_DIMENSION]
        value_head = every_value_row[:, kv_head * HEAD_DIMENSION : (kv_head + 1) * HEAD_DIMENSION]
        scores = (
            jnp.einsum(
                "qrd,kd->rqk", query_head_block, key_head, preferred_element_type=jnp.float32
            )
            * score_scale
        )
        scores = jnp.where(allowed[None], scores, -1e30)
        row_max = jnp.max(scores, axis=-1, keepdims=True)
        weights = jnp.exp(scores - row_max)
        probabilities = weights / jnp.sum(weights, axis=-1, keepdims=True)
        probs_b = probabilities.astype(jnp.bfloat16)
        output_b = jnp.einsum(
            "rqk,kd->qrd", probs_b, value_head, preferred_element_type=jnp.float32
        ).astype(jnp.bfloat16)
        row_delta = jnp.sum(
            gradient_per_head.astype(jnp.float32) * output_b.astype(jnp.float32), axis=-1
        )
        grad_probs = jnp.einsum(
            "qrd,kd->rqk", gradient_per_head, value_head, preferred_element_type=jnp.float32
        )
        grad_scores = (probabilities * (grad_probs - row_delta.T[:, :, None])).astype(jnp.bfloat16)
        grad_query = (
            jnp.einsum("rqk,kd->qrd", grad_scores, key_head, preferred_element_type=jnp.float32)
            * score_scale
        ).astype(jnp.bfloat16)
        key_gradient = (
            jnp.einsum(
                "rqk,qrd->kd", grad_scores, query_head_block, preferred_element_type=jnp.float32
            )
            * score_scale
        )
        value_gradient = jnp.einsum(
            "rqk,qrd->kd", probs_b, gradient_per_head, preferred_element_type=jnp.float32
        )
        out_blocks.append(output_b.reshape(own_len, query_group_width * HEAD_DIMENSION))
        query_grads.append(grad_query.reshape(own_len, query_group_width * HEAD_DIMENSION))
        key_grads.append(key_gradient)
        value_grads.append(value_gradient)
    attn_out = jnp.concatenate(out_blocks, axis=1)
    d_queries = jnp.concatenate(query_grads, axis=1)
    dkeys_all = jnp.concatenate(key_grads, axis=1)
    dvalues_all = jnp.concatenate(value_grads, axis=1)
    branch_key_value_gradient = jnp.stack(
        [dkeys_all[shared_prefix_length:], dvalues_all[shared_prefix_length:]], axis=0
    )
    prefix_part = jnp.stack(
        [
            dkeys_all[:shared_prefix_length].reshape(levels, seg_len, kv_width),
            dvalues_all[:shared_prefix_length].reshape(levels, seg_len, kv_width),
        ],
        axis=1,
    ).astype(jnp.bfloat16)
    prefix_term = prefix_part.astype(jnp.float32)
    targets = jnp.arange(1 * lax.axis_size("branch"))
    matched = lineage[None, :] == targets[:, None]
    summed = lax.psum_scatter(
        jnp.where(matched[:, :, None, None, None], prefix_term[None], 0.0).astype(jnp.bfloat16),
        "branch",
        scatter_dimension=0,
        tiled=True,
    ).astype(jnp.float32)[0]
    return (
        attn_out[None, None],
        d_queries[None, None],
        branch_key_value_gradient[None, None],
        summed[None, None],
    )


def solution(mesh):
    placed = (
        P(("groups", "dp"), "branch", None, "mp"),
        P(("groups", "dp"), "branch", None, None, "mp"),
        P(("groups", "dp"), "branch", None, None, None, "mp"),
        P(("groups", "dp"), "branch", None),
        P(("groups", "dp"), "branch", None),
        P(("groups", "dp"), "branch", None, "mp"),
    )
    return jax.shard_map(
        local,
        mesh=mesh,
        in_specs=placed,
        out_specs=(
            P(("groups", "dp"), "branch", None, "mp"),
            P(("groups", "dp"), "branch", None, "mp"),
            P(("groups", "dp"), "branch", None, None, "mp"),
            P(("groups", "dp"), "branch", None, None, None, "mp"),
        ),
        check_vma=False,
    )
```

profile of v0, /device:TPU:0, one launch (start us, length us, event | category | flops | bytes accessed | tf_op | source)
XLA Modules:
  0.0 140.4 jit_solution(3983517211214474900)
XLA Ops:
  8.6 12.5 %all_gather.7 = bf16[1,4,3]{2,0,1:T(2,128)(2,1)S(1)} all-gather(bf16[1,1,3]{2,0,1:T(2,128)(2,1)S(1)} %bitcast_convert_fusion.1), channel_id=1, replica_groups=mesh['groups'=2,'branch'=4,'dp'=2,'mp'=2] {'branch'}, dimensions={1}, use_global_device_ids=true | all-gather | bytes 30 | tf_op jit(solution)/shard_map/all_gather | solution.py:21
  29.6 1.9 %copy.76 = bf16[1,1,384,2048]{2,3,1,0:T(8,128)(2,1)S(1)} copy(bf16[1,1,384,2048]{3,2,1,0:T(8,128)(2,1)} %param.6) | data formatting | bytes 3145728 | tf_op args[0]
  31.5 2.4 %fusion.58 = (bf16[384,1024]{1,0:T(8,128)(2,1)S(1)}, bf16[384,1024]{1,0:T(8,128)(2,1)}) fusion(bf16[384,2048]{1,0:T(8,128)(2,1)} %bitcast.198), kind=kLoop, calls=%fused_computation.92 | loop fusion | bytes 3145728 | tf_op jit(solution)/shard_map/slice | solution.py:72
  41.2 8.2 %all-gather.2.cloned.1.call-done = bf16[1,4,3,2,128,256]{5,4,3,2,0,1:T(8,128)(2,1)} async-done(((bf16[1,1,3,2,128,256]{5,4,3,2,0,1:T(8,128)(2,1)}), bf16[1,4,3,2,128,256]{5,4,3,2,0,1:T(8,128)(2,1)}) %all-gather.2.cloned.1.call-update) | async-done | bytes 1572880 | tf_op jit(solution)/shard_map/all_gather | solution.py:20
  51.2 8.1 %fusion.65 = (f32[8,384]{1,0:T(8,128)S(1)}, f32[8,384,768]{1,2,0:T(8,128)}) fusion(pred[384,768]{0,1:T(8,128)(4,1)} %pad_add_fusion, bf16[384,8,128]{0,2,1:T(8,128)(2,1)} %bitcast.205, bf16[384,256]{1,0:T(8,128)(2,1)S(1)} %get-tuple-element.26, bf16[384,256]{1,0:T(8,128)(2,1)S(1)} %bitcast.194), kind=kOutput, calls=%fused_computation.99 | convolution fusion | flops 613810944 | bytes 10924032 | tf_op jit(solution)/shard_map/sub | solution.py:85
  59.3 4.6 %fusion.15 = bf16[8,384,768]{1,2,0:T(8,128)(2,1)S(1)} fusion(f32[8,384,768]{1,2,0:T(8,128)} %get-tuple-element.34, f32[8,384]{1,0:T(8,128)S(1)} %get-tuple-element.33), kind=kLoop, calls=%fused_computation.23 | loop fusion | flops 4718592 | bytes 14168064 | tf_op jit(solution)/shard_map/convert_element_type | solution.py:87
  64.0 1.6 %convolution_bitcast_fusion = f32[768,128]{0,1:T(8,128)S(1)} fusion(bf16[8,384,768]{1,2,0:T(8,128)(2,1)S(1)} %fusion.15, bf16[384,8,128]{0,2,1:T(8,128)(2,1)S(1)} %bitcast.183), kind=kOutput, calls=%fused_computation.33 | convolution fusion | flops 603979776 | bytes 5898240 | tf_op jit(solution)/shard_map/rqk,qrd->kd/dot_general | solution.py:108
  65.6 1.7 %multiply_reduce_fusion = (f32[384,8]{0,1:T(8,128)S(1)}, bf16[128,8,384]{2,0,1:T(8,128)(2,1)}) fusion(bf16[384,1024]{0,1:T(8,128)(2,1)S(1)} %copy.88, bf16[8,384,768]{1,2,0:T(8,128)(2,1)S(1)} %fusion.15, bf16[384,256]{0,1:T(8,128)(2,1)S(1)} %bitcast.190, bf16[384,256]{0,1:T(8,128)(2,1)S(1)} %copy.74), kind=kOutput, calls=%fused_computation.28 | convolution fusion | flops 606336000 | bytes 6696960 | tf_op jit(solution)/shard_map/rqk,kd->qrd/dot_general | solution.py:88
  67.4 2.0 %fusion.3 = bf16[8,384,768]{1,2,0:T(8,128)(2,1)S(1)} fusion(f32[8,384]{1,0:T(8,128)S(1)} %bitcast.209, f32[8,384,768]{1,2,0:T(8,128)S(1)} %bitcast.180, f32[8,384]{1,0:T(8,128)S(1)} %get-tuple-element.33, bf16[384,8,128]{0,2,1:T(8,128)(2,1)S(1)} %bitcast.184, bf16[384,256]{0,1:T(8,128)(2,1)S(1)} %bitcast.191, bf16[384,256]{0,1:T(8,128)(2,1)S(1)} %copy.74), kind=kOutput, calls=%fused_computation.4 | convolution fusion | flops 613810176 | bytes 15360000 | tf_op jit(solution)/shard_map/qrd,kd->rqk/dot_general | solution.py:94
  69.4 2.2 %copy-done = bf16[8,384,768]{1,2,0:T(8,128)(2,1)} copy-done((bf16[8,384,768]{1,2,0:T(8,128)(2,1)}, bf16[8,384,768]{1,2,0:T(8,128)(2,1)S(1)}, u32[]{:S(2)}) %copy-start) | copy-done | bytes 4718616
  73.3 8.0 %fusion.70 = (f32[8,384]{1,0:T(8,128)S(1)}, f32[8,384,768]{1,2,0:T(8,128)}) fusion(pred[384,768]{0,1:T(8,128)(4,1)S(1)} %copy-done.7, bf16[384,8,128]{0,2,1:T(8,128)(2,1)} %bitcast.203, bf16[384,256]{1,0:T(8,128)(2,1)S(1)} %bitcast.195, bf16[384,256]{1,0:T(8,128)(2,1)S(1)} %get-tuple-element.26), kind=kOutput, calls=%fused_computation.100 | convolution fusion | flops 613810944 | bytes 10924032 | tf_op jit(solution)/shard_map/sub | solution.py:85
  81.3 4.6 %fusion.14 = bf16[8,384,768]{1,2,0:T(8,128)(2,1)S(1)} fusion(f32[8,384,768]{1,2,0:T(8,128)} %get-tuple-element.36, f32[8,384]{1,0:T(8,128)S(1)} %get-tuple-element.35), kind=kLoop, calls=%fused_computation.22 | loop fusion | flops 4718592 | bytes 14168064 | tf_op jit(solution)/shard_map/convert_element_type | solution.py:87
  85.9 1.7 %multiply_reduce_fusion.1 = (f32[384,8]{0,1:T(8,128)S(1)}, bf16[128,8,384]{2,0,1:T(8,128)(2,1)}) fusion(bf16[384,1024]{0,1:T(8,128)(2,1)S(1)} %copy.83, bf16[8,384,768]{1,2,0:T(8,128)(2,1)S(1)} %fusion.14, bf16[384,256]{0,1:T(8,128)(2,1)S(1)} %copy.74, bf16[384,256]{0,1:T(8,128)(2,1)S(1)} %bitcast.192), kind=kOutput, calls=%fused_computation.30 | convolution fusion | flops 606336000 | bytes 6696960 | tf_op jit(solution)/shard_map/rqk,kd->qrd/dot_general | solution.py:88
  87.7 1.6 %convolution_bitcast_fusion.1 = f32[768,128]{0,1:T(8,128)S(1)} fusion(bf16[8,384,768]{1,2,0:T(8,128)(2,1)S(1)} %fusion.14, bf16[384,8,128]{0,2,1:T(8,128)(2,1)S(1)} %bitcast.181), kind=kOutput, calls=%fused_computation.34 | convolution fusion | flops 603979776 | bytes 5898240 | tf_op jit(solution)/shard_map/rqk,qrd->kd/dot_general | solution.py:108
  89.3 1.8 %fusion.5 = bf16[8,384,768]{1,2,0:T(8,128)(2,1)S(1)} fusion(f32[8,384]{1,0:T(8,128)S(1)} %bitcast.208, f32[8,384,768]{1,2,0:T(8,128)S(1)} %bitcast.178, f32[8,384]{1,0:T(8,128)S(1)} %get-tuple-element.35, bf16[384,8,128]{0,2,1:T(8,128)(2,1)S(1)} %bitcast.182, bf16[384,256]{0,1:T(8,128)(2,1)S(1)} %copy.74, bf16[384,256]{0,1:T(8,128)(2,1)S(1)} %bitcast.193), kind=kOutput, calls=%fused_computation.7 | convolution fusion | flops 613810176 | bytes 15360000 | tf_op jit(solution)/shard_map/qrd,kd->rqk/dot_general | solution.py:94
  91.2 2.1 %copy-done.1 = bf16[8,384,768]{1,2,0:T(8,128)(2,1)} copy-done((bf16[8,384,768]{1,2,0:T(8,128)(2,1)}, bf16[8,384,768]{1,2,0:T(8,128)(2,1)S(1)}, u32[]{:S(2)}) %copy-start.1) | copy-done | bytes 4718616
  93.3 1.6 %fusion.16 = f32[768,128]{0,1:T(8,128)S(1)} fusion(bf16[8,384,768]{1,2,0:T(8,128)(2,1)S(1)} %fusion.5, bf16[384,8,128]{0,2,1:T(8,128)(2,1)S(1)} %bitcast.204), kind=kOutput, calls=%fused_computation.37 | convolution fusion | flops 604078080 | bytes 5898240 | tf_op jit(solution)/shard_map/rqk,qrd->kd/dot_general | solution.py:103
  97.3 4.1 %multiply_convert_fusion = bf16[128,8,384]{2,0,1:T(8,128)(2,1)} fusion(bf16[8,384,768]{1,2,0:T(8,128)(2,1)} %copy-done, bf16[384,256]{1,0:T(8,128)(2,1)S(1)} %get-tuple-element.26, bf16[384,256]{1,0:T(8,128)(2,1)S(1)} %bitcast.196), kind=kOutput, calls=%fused_computation.27 | convolution fusion | flops 605159424 | bytes 5898240 | tf_op jit(solution)/shard_map/rqk,kd->qrd/dot_general | solution.py:99
  104.2 3.1 %multiply_convert_fusion.1 = bf16[128,8,384]{2,0,1:T(8,128)(2,1)S(1)} fusion(bf16[8,384,768]{1,2,0:T(8,128)(2,1)} %copy-done.1, bf16[384,256]{1,0:T(8,128)(2,1)S(1)} %bitcast.197, bf16[384,256]{1,0:T(8,128)(2,1)S(1)} %get-tuple-element.26), kind=kOutput, calls=%fused_computation.29 | convolution fusion | flops 605159424 | bytes 5898240 | tf_op jit(solution)/shard_map/rqk,kd->qrd/dot_general | solution.py:99
  108.5 2.3 %copy.81 = bf16[384,1024]{1,0:T(8,128)(2,1)} copy(bf16[384,1024]{0,1:T(8,128)(2,1)} %bitcast.187) | data formatting | bytes 1572864 | tf_op jit(solution)/shard_map/reshape | solution.py:111
  113.0 2.4 %maximum_bitcast_fusion.1 = bf16[1,1,384,2048]{3,2,1,0:T(8,128)(2,1)} fusion(bf16[384,1024]{1,0:T(8,128)(2,1)S(1)} %copy.94, bf16[384,1024]{1,0:T(8,128)(2,1)} %copy.93), kind=kLoop, calls=%fused_computation.26 | loop fusion | flops 3145728 | bytes 3145728 | tf_op jit(solution)/shard_map/broadcast_in_dim | solution.py:140
  115.4 2.4 %maximum_bitcast_fusion = bf16[1,1,384,2048]{3,2,1,0:T(8,128)(2,1)} fusion(bf16[384,1024]{1,0:T(8,128)(2,1)} %copy.82, bf16[384,1024]{1,0:T(8,128)(2,1)S(1)} %copy-done.2), kind=kLoop, calls=%fused_computation.25 | loop fusion | flops 3145728 | bytes 3145728 | tf_op jit(solution)/shard_map/broadcast_in_dim | solution.py:139
  117.8 13.8 %reduce-scatter.2.cloned.1.call-done = bf16[1,3,2,128,256]{4,3,2,1,0:T(8,128)(2,1)} async-done(((bf16[4,3,2,128,256]{4,3,2,1,0:T(8,128)(2,1)}), bf16[1,3,2,128,256]{4,3,2,1,0:T(8,128)(2,1)}) %reduce-scatter.2.cloned.1.call-update) | async-done | bytes 393232 | tf_op jit(solution)/shard_map/reduce_scatter | solution.py:132
  131.6 1.9 %bitcast_convert_fusion = f32[1,1,3,2,128,256]{5,4,3,2,1,0:T(8,128)} fusion(bf16[1,3,2,128,256]{4,3,2,1,0:T(8,128)(2,1)} %reduce-scatter.2.cloned.1.call-done), kind=kLoop, calls=%fused_computation.62 | loop fusion | flops 196608 | bytes 1179648 | tf_op jit(solution)/shard_map/broadcast_in_dim;squeeze | solution.py:142
  (69 shorter events, 21.3 us)
Async XLA Ops:
  7.2 42.2 %all-gather.2.cloned.1.call-start = ((), (), s32[]{:S(2)}) async-start(), calls=%async_computation.1 | async-start | bytes 1966080 | tf_op jit(solution)/shard_map/all_gather | solution.py:20
  7.9 123.7 %reduce-scatter.2.cloned.1.call-start = ((), (), s32[]{:S(2)}) async-start(), calls=%async_computation.2 | async-start | bytes 1966080 | tf_op jit(solution)/shard_map/reduce_scatter | solution.py:132
  29.6 9.5 %copy-start.8 = (s32[1,1,3]{2,1,0:T(1,128)S(1)}, s32[1,1,3]{2,1,0:T(1,128)}, u32[]{:S(2)}) copy-start(s32[1,1,3]{2,1,0:T(1,128)} %param.9) | copy-start | bytes 40
  59.3 8.0 %slice-start.3 = ((s8[9437184]{0:T(1024)(128)(4,1)}), s8[4194304]{0:T(1024)(128)(4,1)S(1)}, s32[]{:S(2)}) async-start(s8[9437184]{0:T(1024)(128)(4,1)} %bitcast.179), calls=%async_computation.6 | async-start | bytes 8388608
  59.3 8.1 %slice-start.4 = ((s8[9437184]{0:T(1024)(128)(4,1)}), s8[4194304]{0:T(1024)(128)(4,1)S(1)}, s32[]{:S(2)}) async-start(s8[9437184]{0:T(1024)(128)(4,1)} %bitcast.179), calls=%async_computation.7 | async-start | bytes 8388608
  63.9 3.4 %slice-start.5 = ((s8[9437184]{0:T(1024)(128)(4,1)}), s8[1048576]{0:T(1024)(128)(4,1)S(1)}, s32[]{:S(2)}) async-start(s8[9437184]{0:T(1024)(128)(4,1)} %bitcast.179), calls=%async_computation.8 | async-start | bytes 2097152
  67.3 4.3 %copy-start.6 = (bf16[384,1024]{0,1:T(8,128)(2,1)S(1)}, bf16[384,1024]{0,1:T(8,128)(2,1)}, u32[]{:S(2)}) copy-start(bf16[384,1024]{0,1:T(8,128)(2,1)} %get-tuple-element.19) | copy-start | bytes 2359300
  69.4 2.2 %copy-start = (bf16[8,384,768]{1,2,0:T(8,128)(2,1)}, bf16[8,384,768]{1,2,0:T(8,128)(2,1)S(1)}, u32[]{:S(2)}) copy-start(bf16[8,384,768]{1,2,0:T(8,128)(2,1)S(1)} %fusion.3) | copy-start | bytes 14155780
  71.6 1.6 %copy-start.7 = (pred[384,768]{0,1:T(8,128)(4,1)S(1)}, pred[384,768]{0,1:T(8,128)(4,1)}, u32[]{:S(2)}) copy-start(pred[384,768]{0,1:T(8,128)(4,1)} %pad_add_fusion) | copy-start | bytes 884740
  81.3 8.0 %slice-start = ((s8[9437184]{0:T(1024)(128)(4,1)}), s8[4194304]{0:T(1024)(128)(4,1)S(1)}, s32[]{:S(2)}) async-start(s8[9437184]{0:T(1024)(128)(4,1)} %bitcast.177), calls=%async_computation.3 | async-start | bytes 8388608
  81.3 8.0 %slice-start.1 = ((s8[9437184]{0:T(1024)(128)(4,1)}), s8[4194304]{0:T(1024)(128)(4,1)S(1)}, s32[]{:S(2)}) async-start(s8[9437184]{0:T(1024)(128)(4,1)} %bitcast.177), calls=%async_computation.4 | async-start | bytes 8388608
  85.9 3.4 %slice-start.2 = ((s8[9437184]{0:T(1024)(128)(4,1)}), s8[1048576]{0:T(1024)(128)(4,1)S(1)}, s32[]{:S(2)}) async-start(s8[9437184]{0:T(1024)(128)(4,1)} %bitcast.177), calls=%async_computation.5 | async-start | bytes 2097152
  89.3 4.0 %copy-start.5 = (bf16[384,1024]{0,1:T(8,128)(2,1)S(1)}, bf16[384,1024]{0,1:T(8,128)(2,1)}, u32[]{:S(2)}) copy-start(bf16[384,1024]{0,1:T(8,128)(2,1)} %get-tuple-element.18) | copy-start | bytes 2359300
  91.2 2.1 %copy-start.1 = (bf16[8,384,768]{1,2,0:T(8,128)(2,1)}, bf16[8,384,768]{1,2,0:T(8,128)(2,1)S(1)}, u32[]{:S(2)}) copy-start(bf16[8,384,768]{1,2,0:T(8,128)(2,1)S(1)} %fusion.5) | copy-start | bytes 14155780
  94.9 0.8 copy-start.4
  97.3 5.7 %copy-start.3 = (bf16[128,8,384]{2,0,1:T(8,128)(2,1)S(1)}, bf16[128,8,384]{2,0,1:T(8,128)(2,1)}, u32[]{:S(2)}) copy-start(bf16[128,8,384]{2,0,1:T(8,128)(2,1)} %get-tuple-element.38) | copy-start | bytes 2359300
  111.8 3.6 %copy-start.2 = (bf16[384,1024]{1,0:T(8,128)(2,1)S(1)}, bf16[384,1024]{1,0:T(8,128)(2,1)}, u32[]{:S(2)}) copy-start(bf16[384,1024]{1,0:T(8,128)(2,1)} %copy.81) | copy-start | bytes 2359300
Sparse Core Ops, SparseCore 0:
  9.6 39.7 all-gather.1
  97.5 34.1 reduce-scatter.1
where the time goes:
time: 141 us; the launch traced here: 140 us
  matrix products  37.1 us (26%)
  local copies, waits for them, and re-layouts  25.2 us (18%)
  waiting for transfers between devices  22.6 us (16%)
  between operations  22.2 us (16%)
  other arithmetic  20.6 us (15%)
  blocking collectives  12.5 us (9%)
    sub x2, matrix products, local(): weights = jnp.exp(scores - row_max)  16.1 us
    reduce_scatter x1, waiting for transfers between devices, local(): lax.psum_scatter(jnp.where(matched[:, :, None, None, None], prefix_term[N...  13.8 us
    all_gather x1, blocking collectives, local(): lax.all_gather(seg_tiles.astype(jnp.bfloat16), 'branch', axis=1, tiled=True)  12.5 us
    convert_element_type x2, other arithmetic, local(): probs_b = probabilities.astype(jnp.bfloat16)  9.28 us
    all_gather x1, waiting for transfers between devices, local(): part_kv = lax.all_gather(segment_key_values, 'branch', axis=1, tiled=True)  8.16 us
    unnamed x33, local copies, waits for them, and re-layouts  8 us
    dot_general x2, matrix products, local(): jnp.einsum('rqk,kd->qrd', grad_scores, key_head, preferred_element_type=j...  7.24 us
    slice x3, local copies, waits for them, and re-layouts, local(): gradient_row_block[:, head_cols]  4.22 us
  transfers between devices with their start and end apart: 2, of which 2 were waited for; matrix products, arithmetic and copies ran while one was open for 24% of the time, Pallas kernels for 0%

commit v1 on v0

v1 whole, which is shorter than its diff:
```python
import functools
import math

import jax
import jax.numpy as jnp
from jax import lax
from jax.experimental import pallas as pl
from jax.experimental.pallas import tpu as pltpu
from jax.sharding import PartitionSpec as P

QUERY_HEAD_COUNT = 32
KEY_VALUE_HEADS = 4
D = 128
TILE = 64
GROUP = QUERY_HEAD_COUNT // KEY_VALUE_HEADS
SCALE = D ** (-0.5)
LOG2E = 1.0 / math.log(2.0)
MESH = pl.DeviceIdType.MESH
NEG = -1e30
COUNT_ROWS = 16


def kernel(
    n,
    q_hbm,
    do_hbm,
    own_ref,
    seg_ref,
    anc_ref,
    tiles_ref,
    o_hbm,
    dq_hbm,
    down_ref,
    dseg_ref,
    q_v,
    do_v,
    o_v,
    dq_v,
    cur,
    recv,
    gsend,
    grecv,
    k_all,
    v_all,
    k_t,
    v_t,
    acc_k,
    acc_v,
    in_sem,
    out_sem,
    send_sem,
    recv_sem,
    gsend_sem,
    grecv_sem,
):
    levels, seg_len = seg_ref.shape[0], seg_ref.shape[2]
    heads = seg_ref.shape[3] // D
    own_len = own_ref.shape[1]
    pre = levels * seg_len
    width = GROUP * D
    me = lax.axis_index("branch")
    right, left = me + 1, me - 1

    in_copies = []
    for h in range(heads):
        cols = pl.ds(h * width, width)
        for i, (src, dst) in enumerate(((q_hbm, q_v), (do_hbm, do_v))):
            copy = pltpu.make_async_copy(src.at[:, cols], dst.at[:, cols], in_sem.at[h, i])
            copy.start()
            in_copies.append(copy)

    barrier = pltpu.get_barrier_semaphore()

    @pl.when(me > 0)
    def _():
        pl.semaphore_signal(barrier, inc=1, device_id={"branch": left}, device_id_type=MESH)

    @pl.when(me < n - 1)
    def _():
        pl.semaphore_signal(barrier, inc=1, device_id={"branch": right}, device_id_type=MESH)

    @pl.when((me == 0) | (me == n - 1))
    def _():
        pl.semaphore_wait(barrier, 1)

    @pl.when((me > 0) & (me < n - 1))
    def _():
        pl.semaphore_wait(barrier, 2)

    def down_copy(h, l):
        return pltpu.make_async_remote_copy(
            src_ref=cur.at[h, l],
            dst_ref=recv.at[h, l],
            send_sem=send_sem.at[h, l],
            recv_sem=recv_sem.at[h, l],
            device_id={"branch": right},
            device_id_type=MESH,
        )

    def up_copy(h, l):
        return pltpu.make_async_remote_copy(
            src_ref=gsend.at[h, l],
            dst_ref=grecv.at[h, l],
            send_sem=gsend_sem.at[h, l],
            recv_sem=grecv_sem.at[h, l],
            device_id={"branch": left},
            device_id_type=MESH,
        )

    def take_prefix(h):
        cols = slice(h * D, (h + 1) * D)
        for l in range(levels):
            count = jnp.full((COUNT_ROWS, D), tiles_ref[0, 0, l].astype(jnp.float32)).astype(jnp.bfloat16)
            stored = jnp.concatenate([seg_ref[l, 0, :, cols], seg_ref[l, 1, :, cols], count], axis=0)

            @pl.when(me == 0)
            def _():
                cur[h, l] = stored

            @pl.when(me > 0)
            def _():
                down_copy(h, l).wait_recv()
                mine = anc_ref[0, 0, l] == me
                cur[h, l] = jnp.where(mine, stored, recv[h, l])

            @pl.when(me < n - 1)
            def _():
                down_copy(h, l).start()

    def load_own(h):
        cols = slice(h * D, (h + 1) * D)
        k_all[pre:, :] = own_ref[0, :, cols]
        v_all[pre:, :] = own_ref[1, :, cols]
        k_t[:, pre:] = own_ref[0, :, cols].T
        v_t[:, pre:] = own_ref[1, :, cols].T
        acc_k[...] = jnp.zeros_like(acc_k)
        acc_v[...] = jnp.zeros_like(acc_v)

    def load_prefix(h):
        for l in range(levels):
            rows = slice(l * seg_len, (l + 1) * seg_len)
            k = cur[h, l, 0:seg_len, :]
            v = cur[h, l, seg_len : 2 * seg_len, :]
            k_all[rows, :] = k
            v_all[rows, :] = v
            k_t[:, rows] = k.T
            v_t[:, rows] = v.T

    def run_block(h, b, bias):
        rows = slice(b * D, (b + 1) * D)
        nk = pre + (b + 1) * D
        key_at = lax.broadcasted_iota(jnp.int32, (D, 2 * D), 0)
        query_at = lax.broadcasted_iota(jnp.int32, (D, 2 * D), 1)
        visible = key_at <= jnp.where(query_at >= D, query_at - D, query_at)

        def pair(j, carry):
            first = pl.ds(pl.multiple_of(h * width + j * (2 * D), D), D)
            second = pl.ds(pl.multiple_of(h * width + j * (2 * D) + D, D), D)
            qs = jnp.concatenate([q_v[rows, first], q_v[rows, second]], axis=0)
            gs = jnp.concatenate([do_v[rows, first], do_v[rows, second]], axis=0)
            nt = (((1,), (1,)), ((), ()))
            s = lax.dot_general(k_all[0:nk, :], qs, nt, preferred_element_type=jnp.float32)
            parts = []
            for l in range(levels):
                for t in range(seg_len // TILE):
                    lo = l * seg_len + t * TILE
                    part = s[lo : lo + TILE]
                    if t:
                        part = part + bias[l][t - 1]
                    parts.append(part)
            if b:
                parts.append(s[pre : nk - D])
            parts.append(jnp.where(visible, s[nk - D : nk], NEG))
            s = jnp.concatenate(parts, axis=0)
            m = jnp.max(s, axis=0, keepdims=True)
            w = jnp.exp2((s - m) * (SCALE * LOG2E))
            rl = 1.0 / jnp.sum(w, axis=0, keepdims=True)
            o_t = jnp.dot(v_t[:, 0:nk], w.astype(jnp.bfloat16), preferred_element_type=jnp.float32) * rl
            dp = lax.dot_general(v_all[0:nk, :], gs, nt, preferred_element_type=jnp.float32)
            delta = jnp.sum(gs.T.astype(jnp.float32) * o_t, axis=0, keepdims=True)
            p = w * rl
            ds = (p * (dp - delta)).astype(jnp.bfloat16)
            acc_v[0:nk, :] += jnp.dot(p.astype(jnp.bfloat16), gs, preferred_element_type=jnp.float32)
            acc_k[0:nk, :] += jnp.dot(ds, qs, preferred_element_type=jnp.float32)
            dq_t = jnp.dot(k_t[:, 0:nk], ds, preferred_element_type=jnp.float32) * SCALE
            o = o_t.astype(jnp.bfloat16).T
            dq = dq_t.astype(jnp.bfloat16).T
            o_v[rows, first] = o[0:D]
            o_v[rows, second] = o[D : 2 * D]
            dq_v[rows, first] = dq[0:D]
            dq_v[rows, second] = dq[D : 2 * D]
            return carry

        lax.fori_loop(0, GROUP // 2, pair, 0)

    def bias_of(h):
        out = []
        for l in range(levels):
            count = cur[h, l, 2 * seg_len : 2 * seg_len + COUNT_ROWS, :].astype(jnp.float32)[0:1, :]
            count = jnp.concatenate([count, count], axis=1)
            out.append([jnp.where(count > t + 0.5, 0.0, NEG) for t in range(1, seg_len // TILE)])
        return out

    def own_grads(h):
        cols = slice(h * D, (h + 1) * D)
        down_ref[0, :, cols] = acc_k[pre:, :] * SCALE
        down_ref[1, :, cols] = acc_v[pre:, :]

    def stage_grads(h):
        for l in range(levels):
            rows = slice(l * seg_len, (l + 1) * seg_len)
            gsend[h, l, 0:seg_len, :] = (acc_k[rows, :] * SCALE).astype(jnp.bfloat16)
            gsend[h, l, seg_len:, :] = acc_v[rows, :].astype(jnp.bfloat16)

    def pass_grads(h):
        cols = slice(h * D, (h + 1) * D)
        for l in range(levels):
            mine = anc_ref[0, 0, l] == me

            def finish(total):
                kept = jnp.where(mine, total, 0.0)
                dseg_ref[l, 0, :, cols] = kept[0:seg_len]
                dseg_ref[l, 1, :, cols] = kept[seg_len:]
                gsend[h, l] = jnp.where(mine, 0.0, total).astype(jnp.bfloat16)

            @pl.when(me == n - 1)
            def _():
                finish(gsend[h, l].astype(jnp.float32))

            @pl.when(me < n - 1)
            def _():
                up_copy(h, l).wait_recv()
                finish(gsend[h, l].astype(jnp.float32) + grecv[h, l].astype(jnp.float32))

            @pl.when(me > 0)
            def _():
                up_copy(h, l).start()

    out_copies = []

    def write_out(h):
        cols = pl.ds(h * width, width)
        for i, (src, dst) in enumerate(((o_v, o_hbm), (dq_v, dq_hbm))):
            copy = pltpu.make_async_copy(src.at[:, cols], dst.at[:, cols], out_sem.at[h, i])
            copy.start()
            out_copies.append(copy)

    blocks = own_len // D
    for h in range(heads):
        if h == 0:
            take_prefix(0)
        load_own(h)
        load_prefix(h)
        in_copies[2 * h].wait()
        in_copies[2 * h + 1].wait()
        bias = bias_of(h)
        for b in range(blocks):
            run_block(h, b, bias)
            if b == 0 and h + 1 < heads:
                take_prefix(h + 1)
            if h > 0:
                stage = n - 2 - b

                @pl.when((me == stage) if b < blocks - 1 else (me <= stage))
                def _():
                    pass_grads(h - 1)

        write_out(h)
        stage_grads(h)
        if h + 1 < heads:

            @pl.when(me == n - 1)
            def _():
                pass_grads(h)

        own_grads(h)
    pass_grads(heads - 1)

    for copy in out_copies:
        copy.wait()

    @pl.when(me < n - 1)
    def _():
        for h in range(heads):
            for l in range(levels):
                down_copy(h, l).wait_send()

    @pl.when(me > 0)
    def _():
        for h in range(heads):
            for l in range(levels):
                up_copy(h, l).wait_send()


def local(n, queries, own_kv, segment_key_values, ancestors, seg_tiles, grad_out):
    own_len, q_width = queries.shape[2:]
    levels, _, seg_len, kv_width = segment_key_values.shape[2:]
    heads = kv_width // D
    keys = levels * seg_len + own_len
    vmem = pl.BlockSpec(memory_space=pltpu.VMEM)
    smem = pl.BlockSpec(memory_space=pltpu.SMEM)
    hbm = pl.BlockSpec(memory_space=pl.ANY)
    bf16, f32 = jnp.bfloat16, jnp.float32
    rows_of = pltpu.VMEM((own_len, q_width), bf16)
    out = pl.pallas_call(
        functools.partial(kernel, n),
        out_shape=(
            jax.ShapeDtypeStruct((own_len, q_width), bf16),
            jax.ShapeDtypeStruct((own_len, q_width), bf16),
            jax.ShapeDtypeStruct((2, own_len, kv_width), f32),
            jax.ShapeDtypeStruct((levels, 2, seg_len, kv_width), f32),
        ),
        in_specs=[hbm, hbm, vmem, vmem, smem, smem],
        out_specs=(hbm, hbm, vmem, vmem),
        scratch_shapes=[
            rows_of,
            rows_of,
            rows_of,
            rows_of,
            pltpu.VMEM((heads, levels, 2 * seg_len + COUNT_ROWS, D), bf16),
            pltpu.VMEM((heads, levels, 2 * seg_len + COUNT_ROWS, D), bf16),
            pltpu.VMEM((heads, levels, 2 * seg_len, D), bf16),
            pltpu.VMEM((heads, levels, 2 * seg_len, D), bf16),
            pltpu.VMEM((keys, D), bf16),
            pltpu.VMEM((keys, D), bf16),
            pltpu.VMEM((D, keys), bf16),
            pltpu.VMEM((D, keys), bf16),
            pltpu.VMEM((keys, D), f32),
            pltpu.VMEM((keys, D), f32),
            pltpu.SemaphoreType.DMA((heads, 2)),
            pltpu.SemaphoreType.DMA((heads, 2)),
            pltpu.SemaphoreType.DMA((heads, levels)),
            pltpu.SemaphoreType.DMA((heads, levels)),
            pltpu.SemaphoreType.DMA((heads, levels)),
            pltpu.SemaphoreType.DMA((heads, levels)),
        ],
        compiler_params=pltpu.CompilerParams(
            collective_id=0, has_side_effects=True, vmem_limit_bytes=48 * 1024 * 1024
        ),
    )(queries[0, 0], grad_out[0, 0], own_kv[0, 0], segment_key_values[0, 0], ancestors, seg_tiles)
    return tuple(x[None, None] for x in out)


def solution(mesh):
    placed = (
        P(("groups", "dp"), "branch", None, "mp"),
        P(("groups", "dp"), "branch", None, None, "mp"),
        P(("groups", "dp"), "branch", None, None, None, "mp"),
        P(("groups", "dp"), "branch", None),
        P(("groups", "dp"), "branch", None),
        P(("groups", "dp"), "branch", None, "mp"),
    )
    return jax.shard_map(
        functools.partial(local, mesh.shape["branch"]),
        mesh=mesh,
        in_specs=placed,
        out_specs=(
            P(("groups", "dp"), "branch", None, "mp"),
            P(("groups", "dp"), "branch", None, "mp"),
            P(("groups", "dp"), "branch", None, None, "mp"),
            P(("groups", "dp"), "branch", None, None, None, "mp"),
        ),
        check_vma=False,
    )
```

time: 141 us -> 63.5 us (0.45)
  Pallas kernels: 0 us -> 55.3 us
  matrix products: 37.1 us -> 0 us
  waiting for transfers between devices: 22.6 us -> 0 us
  between operations: 22.2 us -> 0.65 us
  other arithmetic: 20.6 us -> 0 us
  local copies, waits for them, and re-layouts: 25.2 us -> 7.34 us
  blocking collectives: 12.5 us -> 0 us
    pallas_call x0 -> x1, Pallas kernels: none -> 55.3 us  [local(): pl.pallas_call(functools.partial(kernel, n), out_shape=(jax.ShapeDtypeStr...]
    dot_general x10 -> x0, matrix products: 21 us -> none  [the longest x2 7.24 us: local(): jnp.einsum('rqk,kd->qrd', grad_scores, key_head, preferred_element_type=j...]
    sub x2 -> x0, matrix products: 16.1 us -> none  [local(): weights = jnp.exp(scores - row_max)]
    reduce_scatter x1 -> x0, waiting for transfers between devices: 13.8 us -> none  [local(): lax.psum_scatter(jnp.where(matched[:, :, None, None, None], prefix_term[N...]
    all_gather x1 -> x0, blocking collectives: 12.5 us -> none  [local(): lax.all_gather(seg_tiles.astype(jnp.bfloat16), 'branch', axis=1, tiled=True)]
    convert_element_type x4 -> x0, other arithmetic: 11.6 us -> none  [the longest x2 9.28 us: local(): probs_b = probabilities.astype(jnp.bfloat16)]
    slice x11 -> x0, local copies, waits for them, and re-layouts: 9.82 us -> none  [the longest x3 4.22 us: local(): gradient_row_block[:, head_cols]]
    all_gather x1 -> x0, waiting for transfers between devices: 8.16 us -> none  [local(): part_kv = lax.all_gather(segment_key_values, 'branch', axis=1, tiled=True)]
  transfers between devices with their start and end apart: 2 -> 0, of which waited for: 2 -> 0; matrix products, arithmetic and copies ran while one was open for 24% -> 0% of each run, Pallas kernels for 0% -> 0%
where the time goes in v1:
time: 63.5 us; the launch traced here: 63.3 us
  Pallas kernels  55.3 us (87%)
  local copies, waits for them, and re-layouts  7.34 us (12%)
  between operations  0.65 us (1%)
    pallas_call x1, Pallas kernels, local(): pl.pallas_call(functools.partial(kernel, n), out_shape=(jax.ShapeDtypeStr...  55.3 us
    unnamed x12, local copies, waits for them, and re-layouts  7.34 us

profile of v1, /device:TPU:0, one launch (start us, length us, event | category | flops | bytes accessed | tf_op | source)
XLA Modules:
  0.0 63.3 jit_solution(1545804063183257396)
XLA Ops:
  0.6 0.0 copy-start
  0.6 1.0 %copy-done = bf16[1,1,2,384,256]{4,3,2,1,0:T(8,128)(2,1)S(1)} copy-done((bf16[1,1,2,384,256]{4,3,2,1,0:T(8,128)(2,1)S(1)}, bf16[1,1,2,384,256]{4,3,2,1,0:T(8,128)(2,1)}, u32[]{:S(2)}) %copy-start) | copy-done | bytes 393240
  1.6 0.0 copy-start.1
  1.6 1.0 %copy-done.1 = bf16[1,1,3,2,128,256]{5,4,3,2,1,0:T(8,128)(2,1)S(1)} copy-done((bf16[1,1,3,2,128,256]{5,4,3,2,1,0:T(8,128)(2,1)S(1)}, bf16[1,1,3,2,128,256]{5,4,3,2,1,0:T(8,128)(2,1)}, u32[]{:S(2)}) %copy-start.1) | copy-done | bytes 393240
  2.6 0.0 copy-start.2
  2.6 0.7 %copy-done.2 = s32[1,1,3]{2,1,0:T(1,128)S(1)} copy-done((s32[1,1,3]{2,1,0:T(1,128)S(1)}, s32[1,1,3]{2,1,0:T(1,128)}, u32[]{:S(2)}) %copy-start.2) | copy-done | bytes 36
  3.3 0.0 copy-start.3
  3.3 0.7 %copy-done.3 = s32[1,1,3]{2,1,0:T(1,128)S(1)} copy-done((s32[1,1,3]{2,1,0:T(1,128)S(1)}, s32[1,1,3]{2,1,0:T(1,128)}, u32[]{:S(2)}) %copy-start.3) | copy-done | bytes 36
  3.9 55.3 %shard_map.93 = (bf16[384,2048]{1,0:T(8,128)(2,1)S(1)}, bf16[384,2048]{1,0:T(8,128)(2,1)S(1)}, f32[2,384,256]{2,1,0:T(8,128)S(1)}, f32[3,2,128,256]{3,2,1,0:T(8,128)S(1)}) custom-call(bf16[384,2048]{1,0:T(8,128)(2,1)} %bitcast.14, bf16[384,2048]{1,0:T(8,128)(2,1)} %bitcast.15, bf16[2,384,256]{2,1,0:T(8,128)(2,1)S(1)} %bitcast.12, ...), custom_call_target="tpu_custom_call" | custom-call | tf_op jit(solution)/shard_map/pallas_call | solution.py:305
  59.3 1.1 %copy.14 = bf16[1,1,384,2048]{3,2,1,0:T(8,128)(2,1)} copy(bf16[1,1,384,2048]{3,2,1,0:T(8,128)(2,1)S(1)} %bitcast.9) | data formatting | bytes 3145728
  60.4 1.1 %copy.15 = bf16[1,1,384,2048]{3,2,1,0:T(8,128)(2,1)} copy(bf16[1,1,384,2048]{3,2,1,0:T(8,128)(2,1)S(1)} %bitcast.8) | data formatting | bytes 3145728
  61.6 0.9 %copy.16 = f32[1,1,2,384,256]{4,3,2,1,0:T(8,128)} copy(f32[1,1,2,384,256]{4,3,2,1,0:T(8,128)S(1)} %bitcast.11) | data formatting | bytes 1572864
  62.4 0.9 %copy.17 = f32[1,1,3,2,128,256]{5,4,3,2,1,0:T(8,128)} copy(f32[1,1,3,2,128,256]{5,4,3,2,1,0:T(8,128)S(1)} %bitcast.10) | data formatting | bytes 1572864
Async XLA Ops:
  0.6 1.0 %copy-start = (bf16[1,1,2,384,256]{4,3,2,1,0:T(8,128)(2,1)S(1)}, bf16[1,1,2,384,256]{4,3,2,1,0:T(8,128)(2,1)}, u32[]{:S(2)}) copy-start(bf16[1,1,2,384,256]{4,3,2,1,0:T(8,128)(2,1)} %param.7) | copy-start | bytes 1179652
  1.6 1.0 %copy-start.1 = (bf16[1,1,3,2,128,256]{5,4,3,2,1,0:T(8,128)(2,1)S(1)}, bf16[1,1,3,2,128,256]{5,4,3,2,1,0:T(8,128)(2,1)}, u32[]{:S(2)}) copy-start(bf16[1,1,3,2,128,256]{5,4,3,2,1,0:T(8,128)(2,1)} %param.8) | copy-start | bytes 1179652
  2.6 0.7 %copy-start.2 = (s32[1,1,3]{2,1,0:T(1,128)S(1)}, s32[1,1,3]{2,1,0:T(1,128)}, u32[]{:S(2)}) copy-start(s32[1,1,3]{2,1,0:T(1,128)} %anc_ref.1) | copy-start | bytes 40
  3.3 0.7 %copy-start.3 = (s32[1,1,3]{2,1,0:T(1,128)S(1)}, s32[1,1,3]{2,1,0:T(1,128)}, u32[]{:S(2)}) copy-start(s32[1,1,3]{2,1,0:T(1,128)} %tiles_ref.1) | copy-start | bytes 40

commit v2 on v1

v2 whole, which is shorter than its diff:
```python
import functools
import math

import jax
import jax.numpy as jnp
from jax import lax
from jax.experimental import pallas as pl
from jax.experimental.pallas import tpu as pltpu
from jax.sharding import PartitionSpec as P

QUERY_HEAD_COUNT = 32
KEY_VALUE_HEADS = 4
D = 128
TILE = 64
GROUP = QUERY_HEAD_COUNT // KEY_VALUE_HEADS
SCALE = D ** (-0.5)
LOG2E = 1.0 / math.log(2.0)
MESH = pl.DeviceIdType.MESH
NEG = -1e30
COUNT_ROWS = 16


def kernel(
    n,
    q_hbm,
    do_hbm,
    own_hbm,
    seg_hbm,
    anc_hbm,
    tiles_hbm,
    o_hbm,
    dq_hbm,
    down_ref,
    dseg_ref,
    q_v,
    do_v,
    o_v,
    dq_v,
    own_ref,
    seg_ref,
    anc_ref,
    tiles_ref,
    cur,
    recv,
    gsend,
    grecv,
    k_all,
    v_all,
    k_t,
    v_t,
    acc_k,
    acc_v,
    small_sem,
    in_sem,
    out_sem,
    send_sem,
    recv_sem,
    gsend_sem,
    grecv_sem,
):
    levels, seg_len = seg_ref.shape[0], seg_ref.shape[2]
    heads = seg_ref.shape[3] // D
    own_len = own_ref.shape[1]
    pre = levels * seg_len
    width = GROUP * D
    me = lax.axis_index("branch")
    right, left = me + 1, me - 1

    small = []
    for i, (src, dst) in enumerate(
        ((anc_hbm, anc_ref), (tiles_hbm, tiles_ref), (seg_hbm, seg_ref), (own_hbm, own_ref))
    ):
        copy = pltpu.make_async_copy(src, dst, small_sem.at[i])
        copy.start()
        small.append(copy)
    in_copies = []
    for h in range(heads):
        cols = pl.ds(h * width, width)
        for i, (src, dst) in enumerate(((q_hbm, q_v), (do_hbm, do_v))):
            copy = pltpu.make_async_copy(src.at[:, cols], dst.at[:, cols], in_sem.at[h, i])
            copy.start()
            in_copies.append(copy)

    barrier = pltpu.get_barrier_semaphore()

    @pl.when(me > 0)
    def _():
        pl.semaphore_signal(barrier, inc=1, device_id={"branch": left}, device_id_type=MESH)

    @pl.when(me < n - 1)
    def _():
        pl.semaphore_signal(barrier, inc=1, device_id={"branch": right}, device_id_type=MESH)

    @pl.when((me == 0) | (me == n - 1))
    def _():
        pl.semaphore_wait(barrier, 1)

    @pl.when((me > 0) & (me < n - 1))
    def _():
        pl.semaphore_wait(barrier, 2)

    def down_copy(h, l, c):
        return pltpu.make_async_remote_copy(
            src_ref=cur.at[h, l, c],
            dst_ref=recv.at[h, l, c],
            send_sem=send_sem.at[h, l, c],
            recv_sem=recv_sem.at[h, l, c],
            device_id={"branch": right},
            device_id_type=MESH,
        )

    def up_copy(h, l, c):
        return pltpu.make_async_remote_copy(
            src_ref=gsend.at[h, l, c],
            dst_ref=grecv.at[h, l, c],
            send_sem=gsend_sem.at[h, l, c],
            recv_sem=grecv_sem.at[h, l, c],
            device_id={"branch": left},
            device_id_type=MESH,
        )

    def first_prefix(h):
        cols = slice(h * D, (h + 1) * D)

        @pl.when(me == 0)
        def _():
            for c in range(2):
                for l in range(levels):
                    cur[h, l, c] = stored_of(l, c, cols)
                    down_copy(h, l, c).start()

    def stored_of(l, c, cols):
        count = jnp.full((COUNT_ROWS, D), tiles_ref[0, 0, l].astype(jnp.float32)).astype(jnp.bfloat16)
        return jnp.concatenate([seg_ref[l, c, :, cols], count], axis=0)

    def take_prefix(h, c):
        cols = slice(h * D, (h + 1) * D)
        for l in range(levels):

            @pl.when(me > 0)
            def _():
                down_copy(h, l, c).wait_recv()
                mine = anc_ref[0, 0, l] == me
                cur[h, l, c] = jnp.where(mine, stored_of(l, c, cols), recv[h, l, c])

            @pl.when((me > 0) & (me < n - 1))
            def _():
                down_copy(h, l, c).start()

    def load_own(h):
        cols = slice(h * D, (h + 1) * D)
        k_all[pre:, :] = own_ref[0, :, cols]
        v_all[pre:, :] = own_ref[1, :, cols]
        k_t[:, pre:] = own_ref[0, :, cols].T
        v_t[:, pre:] = own_ref[1, :, cols].T
        acc_k[...] = jnp.zeros_like(acc_k)
        acc_v[...] = jnp.zeros_like(acc_v)

    def load_prefix(h, c):
        rows_ref, turned_ref = ((k_all, k_t), (v_all, v_t))[c]
        for l in range(levels):
            rows = slice(l * seg_len, (l + 1) * seg_len)
            x = cur[h, l, c, 0:seg_len, :]
            rows_ref[rows, :] = x
            turned_ref[:, rows] = x.T

    nt = (((1,), (1,)), ((), ()))
    key_at = lax.broadcasted_iota(jnp.int32, (D, D), 0)
    query_at = lax.broadcasted_iota(jnp.int32, (D, D), 1)
    unseen = jnp.where(key_at <= query_at, 0.0, NEG)
    unseen = jnp.concatenate([unseen] * GROUP, axis=1)

    def operands(h, b):
        rows = slice(b * D, (b + 1) * D)
        cols = [slice(h * width + i * D, h * width + (i + 1) * D) for i in range(GROUP)]
        qs = jnp.concatenate([q_v[rows, c] for c in cols], axis=0)
        gs = jnp.concatenate([do_v[rows, c] for c in cols], axis=0)
        return rows, cols, qs, gs

    def own_scores(h, b):
        _, _, qs, gs = operands(h, b)
        nk = pre + (b + 1) * D
        s = lax.dot_general(k_all[pre:nk, :], qs, nt, preferred_element_type=jnp.float32)
        diagonal = s[b * D :] + unseen
        s = jnp.concatenate([s[: b * D], diagonal], axis=0) if b else diagonal
        dp = lax.dot_general(v_all[pre:nk, :], gs, nt, preferred_element_type=jnp.float32)
        return s, dp

    def prefix_scores(h, b, bias):
        _, _, qs, _ = operands(h, b)
        s = lax.dot_general(k_all[0:pre, :], qs, nt, preferred_element_type=jnp.float32)
        parts = []
        for l in range(levels):
            for t in range(seg_len // TILE):
                lo = l * seg_len + t * TILE
                part = s[lo : lo + TILE]
                parts.append(part + bias[l][t - 1] if t else part)
        return jnp.concatenate(parts, axis=0)

    def run_block(h, b, prefix_s, own_part):
        rows, cols, qs, gs = operands(h, b)
        nk = pre + (b + 1) * D
        own_s, own_dp = own_part
        s = jnp.concatenate([prefix_s, own_s], axis=0)
        m = jnp.max(s, axis=0, keepdims=True)
        w = jnp.exp2((s - m) * (SCALE * LOG2E))
        rl = 1.0 / jnp.sum(w, axis=0, keepdims=True)
        o_t = jnp.dot(v_t[:, 0:nk], w.astype(jnp.bfloat16), preferred_element_type=jnp.float32) * rl
        dp = lax.dot_general(v_all[0:pre, :], gs, nt, preferred_element_type=jnp.float32)
        dp = jnp.concatenate([dp, own_dp], axis=0)
        delta = jnp.sum(gs.T.astype(jnp.float32) * o_t, axis=0, keepdims=True)
        p = w * rl
        ds = (p * (dp - delta)).astype(jnp.bfloat16)
        pb = p.astype(jnp.bfloat16)
        acc_v[0:pre, :] += jnp.dot(pb[0:pre], gs, preferred_element_type=jnp.float32)
        acc_k[0:pre, :] += jnp.dot(ds[0:pre], qs, preferred_element_type=jnp.float32)
        o = o_t.astype(jnp.bfloat16).T
        for i, c in enumerate(cols):
            o_v[rows, c] = o[i * D : (i + 1) * D]

        def rest():
            _, _, qs, gs = operands(h, b)
            acc_v[pre:nk, :] += jnp.dot(pb[pre:], gs, preferred_element_type=jnp.float32)
            acc_k[pre:nk, :] += jnp.dot(ds[pre:], qs, preferred_element_type=jnp.float32)
            dq_t = jnp.dot(k_t[:, 0:nk], ds, preferred_element_type=jnp.float32) * SCALE
            dq = dq_t.astype(jnp.bfloat16).T
            for i, c in enumerate(cols):
                dq_v[rows, c] = dq[i * D : (i + 1) * D]

        return rest

    def bias_of(h):
        out = []
        for l in range(levels):
            count = cur[h, l, 0, seg_len : seg_len + COUNT_ROWS, :].astype(jnp.float32)[0:1, :]
            count = jnp.concatenate([count] * GROUP, axis=1)
            out.append([jnp.where(count > t + 0.5, 0.0, NEG) for t in range(1, seg_len // TILE)])
        return out

    def own_grads(h):
        cols = slice(h * D, (h + 1) * D)
        down_ref[0, :, cols] = acc_k[pre:, :] * SCALE
        down_ref[1, :, cols] = acc_v[pre:, :]

    def pass_grads(h):
        cols = slice(h * D, (h + 1) * D)
        for l in range(levels):
            mine = anc_ref[0, 0, l] == me
            for c in range(2):

                def finish(total):
                    dseg_ref[l, c, :, cols] = jnp.where(mine, total, 0.0)
                    gsend[h, l, c] = jnp.where(mine, 0.0, total).astype(jnp.bfloat16)

                @pl.when(me == n - 1)
                def _():
                    finish(gsend[h, l, c].astype(jnp.float32))

                @pl.when(me < n - 1)
                def _():
                    up_copy(h, l, c).wait_recv()
                    finish(gsend[h, l, c].astype(jnp.float32) + grecv[h, l, c].astype(jnp.float32))

                @pl.when(me > 0)
                def _():
                    up_copy(h, l, c).start()

    def stage_grads(h):
        for l in range(levels):
            rows = slice(l * seg_len, (l + 1) * seg_len)
            gsend[h, l, 0] = (acc_k[rows, :] * SCALE).astype(jnp.bfloat16)
            gsend[h, l, 1] = acc_v[rows, :].astype(jnp.bfloat16)

        @pl.when(me == n - 1)
        def _():
            pass_grads(h)

    out_copies = []

    def write_out(h, i):
        cols = pl.ds(h * width, width)
        src, dst = ((o_v, o_hbm), (dq_v, dq_hbm))[i]
        copy = pltpu.make_async_copy(src.at[:, cols], dst.at[:, cols], out_sem.at[h, i])
        copy.start()
        out_copies.append(copy)

    blocks = own_len // D
    for copy in small:
        copy.wait()
    for h in range(heads):
        first_prefix(h)
    for h in range(heads):
        last = h == heads - 1
        load_own(h)
        in_copies[2 * h].wait()
        in_copies[2 * h + 1].wait()
        own_parts = [own_scores(h, b) for b in range(blocks)]
        if h == 0:
            take_prefix(0, 0)
        load_prefix(h, 0)
        bias = bias_of(h)
        prefix_parts = [prefix_scores(h, b, bias) for b in range(blocks)]
        if h == 0:
            take_prefix(0, 1)
        load_prefix(h, 1)
        rests = []
        for b in range(blocks):
            rests.append(run_block(h, b, prefix_parts[b], own_parts[b]))
            if not last:
                rests.pop()()
            if b == 0 and not last:
                take_prefix(h + 1, 0)
                take_prefix(h + 1, 1)
            if b == 1 and h > 0:

                @pl.when(me == n - 2)
                def _():
                    pass_grads(h - 1)

        stage_grads(h)
        write_out(h, 0)
        for rest in rests:
            rest()
        write_out(h, 1)
        own_grads(h)

    @pl.when(me < n - 2)
    def _():
        for h in range(heads - 1):
            pass_grads(h)

    @pl.when(me < n - 1)
    def _():
        pass_grads(heads - 1)

    for copy in out_copies:
        copy.wait()

    pieces = [(h, l, c) for h in range(heads) for l in range(levels) for c in range(2)]

    @pl.when(me < n - 1)
    def _():
        for piece in pieces:
            down_copy(*piece).wait_send()

    @pl.when(me > 0)
    def _():
        for piece in pieces:
            up_copy(*piece).wait_send()


def local(n, queries, own_kv, segment_key_values, ancestors, seg_tiles, grad_out):
    own_len, q_width = queries.shape[2:]
    levels, _, seg_len, kv_width = segment_key_values.shape[2:]
    heads = kv_width // D
    keys = levels * seg_len + own_len
    vmem = pl.BlockSpec(memory_space=pltpu.VMEM)
    hbm = pl.BlockSpec(memory_space=pl.ANY)
    bf16, f32 = jnp.bfloat16, jnp.float32
    rows_of = pltpu.VMEM((own_len, q_width), bf16)
    out = pl.pallas_call(
        functools.partial(kernel, n),
        out_shape=(
            jax.ShapeDtypeStruct((own_len, q_width), bf16),
            jax.ShapeDtypeStruct((own_len, q_width), bf16),
            jax.ShapeDtypeStruct((2, own_len, kv_width), f32),
            jax.ShapeDtypeStruct((levels, 2, seg_len, kv_width), f32),
        ),
        in_specs=[pl.BlockSpec(memory_space=pltpu.HBM)] * 6,
        out_specs=(hbm, hbm, vmem, vmem),
        scratch_shapes=[
            rows_of,
            rows_of,
            rows_of,
            rows_of,
            pltpu.VMEM((2, own_len, kv_width), bf16),
            pltpu.VMEM((levels, 2, seg_len, kv_width), bf16),
            pltpu.SMEM((1, 1, levels), jnp.int32),
            pltpu.SMEM((1, 1, levels), jnp.int32),
            pltpu.VMEM((heads, levels, 2, seg_len + COUNT_ROWS, D), bf16),
            pltpu.VMEM((heads, levels, 2, seg_len + COUNT_ROWS, D), bf16),
            pltpu.VMEM((heads, levels, 2, seg_len, D), bf16),
            pltpu.VMEM((heads, levels, 2, seg_len, D), bf16),
            pltpu.VMEM((keys, D), bf16),
            pltpu.VMEM((keys, D), bf16),
            pltpu.VMEM((D, keys), bf16),
            pltpu.VMEM((D, keys), bf16),
            pltpu.VMEM((keys, D), f32),
            pltpu.VMEM((keys, D), f32),
            pltpu.SemaphoreType.DMA((4,)),
            pltpu.SemaphoreType.DMA((heads, 2)),
            pltpu.SemaphoreType.DMA((heads, 2)),
            pltpu.SemaphoreType.DMA((heads, levels, 2)),
            pltpu.SemaphoreType.DMA((heads, levels, 2)),
            pltpu.SemaphoreType.DMA((heads, levels, 2)),
            pltpu.SemaphoreType.DMA((heads, levels, 2)),
        ],
        compiler_params=pltpu.CompilerParams(
            collective_id=0, has_side_effects=True, vmem_limit_bytes=48 * 1024 * 1024
        ),
    )(queries[0, 0], grad_out[0, 0], own_kv[0, 0], segment_key_values[0, 0], ancestors, seg_tiles)
    return tuple(x[None, None] for x in out)


def solution(mesh):
    placed = (
        P(("groups", "dp"), "branch", None, "mp"),
        P(("groups", "dp"), "branch", None, None, "mp"),
        P(("groups", "dp"), "branch", None, None, None, "mp"),
        P(("groups", "dp"), "branch", None),
        P(("groups", "dp"), "branch", None),
        P(("groups", "dp"), "branch", None, "mp"),
    )
    return jax.shard_map(
        functools.partial(local, mesh.shape["branch"]),
        mesh=mesh,
        in_specs=placed,
        out_specs=(
            P(("groups", "dp"), "branch", None, "mp"),
            P(("groups", "dp"), "branch", None, "mp"),
            P(("groups", "dp"), "branch", None, None, "mp"),
            P(("groups", "dp"), "branch", None, None, None, "mp"),
        ),
        check_vma=False,
    )
```

time: 63.5 us -> 50.9 us (0.80)
  Pallas kernels: 55.3 us -> 42.7 us
    pallas_call x1, Pallas kernels: 55.3 us -> 42.7 us  [local(): pl.pallas_call(functools.partial(kernel, n), out_shape=(jax.ShapeDtypeStr...]
where the time goes in v2:
time: 50.9 us; the launch traced here: 50.7 us
  Pallas kernels  42.7 us (84%)
  local copies, waits for them, and re-layouts  7.34 us (14%)
  between operations  0.65 us (1%)
    pallas_call x1, Pallas kernels, local(): pl.pallas_call(functools.partial(kernel, n), out_shape=(jax.ShapeDtypeStr...  42.7 us
    unnamed x12, local copies, waits for them, and re-layouts  7.34 us

profile of v2, /device:TPU:0, one launch (start us, length us, event | category | flops | bytes accessed | tf_op | source)
XLA Modules:
  0.0 50.7 jit_solution(10384531074691832175)
XLA Ops:
  0.6 0.0 copy-start
  0.6 1.0 %copy-done = bf16[1,1,2,384,256]{4,3,2,1,0:T(8,128)(2,1)S(1)} copy-done((bf16[1,1,2,384,256]{4,3,2,1,0:T(8,128)(2,1)S(1)}, bf16[1,1,2,384,256]{4,3,2,1,0:T(8,128)(2,1)}, u32[]{:S(2)}) %copy-start) | copy-done | bytes 393240
  1.6 0.0 copy-start.1
  1.6 1.0 %copy-done.1 = bf16[1,1,3,2,128,256]{5,4,3,2,1,0:T(8,128)(2,1)S(1)} copy-done((bf16[1,1,3,2,128,256]{5,4,3,2,1,0:T(8,128)(2,1)S(1)}, bf16[1,1,3,2,128,256]{5,4,3,2,1,0:T(8,128)(2,1)}, u32[]{:S(2)}) %copy-start.1) | copy-done | bytes 393240
  2.6 0.0 copy-start.2
  2.6 0.7 %copy-done.2 = s32[1,1,3]{2,1,0:T(1,128)S(1)} copy-done((s32[1,1,3]{2,1,0:T(1,128)S(1)}, s32[1,1,3]{2,1,0:T(1,128)}, u32[]{:S(2)}) %copy-start.2) | copy-done | bytes 36
  3.3 0.0 copy-start.3
  3.3 0.7 %copy-done.3 = s32[1,1,3]{2,1,0:T(1,128)S(1)} copy-done((s32[1,1,3]{2,1,0:T(1,128)S(1)}, s32[1,1,3]{2,1,0:T(1,128)}, u32[]{:S(2)}) %copy-start.3) | copy-done | bytes 36
  3.9 42.7 %shard_map.93 = (bf16[384,2048]{1,0:T(8,128)(2,1)S(1)}, bf16[384,2048]{1,0:T(8,128)(2,1)S(1)}, f32[2,384,256]{2,1,0:T(8,128)S(1)}, f32[3,2,128,256]{3,2,1,0:T(8,128)S(1)}) custom-call(bf16[384,2048]{1,0:T(8,128)(2,1)} %bitcast.14, bf16[384,2048]{1,0:T(8,128)(2,1)} %bitcast.15, bf16[2,384,256]{2,1,0:T(8,128)(2,1)S(1)} %bitcast.12, ...), custom_call_target="tpu_custom_call" | custom-call | tf_op jit(solution)/shard_map/pallas_call | solution.py:361
  46.7 1.1 %copy.14 = bf16[1,1,384,2048]{3,2,1,0:T(8,128)(2,1)} copy(bf16[1,1,384,2048]{3,2,1,0:T(8,128)(2,1)S(1)} %bitcast.9) | data formatting | bytes 3145728
  47.8 1.1 %copy.15 = bf16[1,1,384,2048]{3,2,1,0:T(8,128)(2,1)} copy(bf16[1,1,384,2048]{3,2,1,0:T(8,128)(2,1)S(1)} %bitcast.8) | data formatting | bytes 3145728
  48.9 0.9 %copy.16 = f32[1,1,2,384,256]{4,3,2,1,0:T(8,128)} copy(f32[1,1,2,384,256]{4,3,2,1,0:T(8,128)S(1)} %bitcast.11) | data formatting | bytes 1572864
  49.8 0.9 %copy.17 = f32[1,1,3,2,128,256]{5,4,3,2,1,0:T(8,128)} copy(f32[1,1,3,2,128,256]{5,4,3,2,1,0:T(8,128)S(1)} %bitcast.10) | data formatting | bytes 1572864
Async XLA Ops:
  0.6 1.0 %copy-start = (bf16[1,1,2,384,256]{4,3,2,1,0:T(8,128)(2,1)S(1)}, bf16[1,1,2,384,256]{4,3,2,1,0:T(8,128)(2,1)}, u32[]{:S(2)}) copy-start(bf16[1,1,2,384,256]{4,3,2,1,0:T(8,128)(2,1)} %param.7) | copy-start | bytes 1179652
  1.6 1.0 %copy-start.1 = (bf16[1,1,3,2,128,256]{5,4,3,2,1,0:T(8,128)(2,1)S(1)}, bf16[1,1,3,2,128,256]{5,4,3,2,1,0:T(8,128)(2,1)}, u32[]{:S(2)}) copy-start(bf16[1,1,3,2,128,256]{5,4,3,2,1,0:T(8,128)(2,1)} %param.8) | copy-start | bytes 1179652
  2.6 0.7 %copy-start.2 = (s32[1,1,3]{2,1,0:T(1,128)S(1)}, s32[1,1,3]{2,1,0:T(1,128)}, u32[]{:S(2)}) copy-start(s32[1,1,3]{2,1,0:T(1,128)} %anc_hbm.1) | copy-start | bytes 40
  3.3 0.7 %copy-start.3 = (s32[1,1,3]{2,1,0:T(1,128)S(1)}, s32[1,1,3]{2,1,0:T(1,128)}, u32[]{:S(2)}) copy-start(s32[1,1,3]{2,1,0:T(1,128)} %tiles_hbm.1) | copy-start | bytes 40
